TPU v7x, 128 devices: a whole 4x4x4 slice. The times are simulated.
128 devices in a mesh: dp: 16 (over x_lo, y, core), tensor: 8 (over x_hi, z).
Axes of the slice: x: 4 (x_hi: 2, x_lo: 2; x = x_hi * 2 + x_lo), y: 4, z: 4, core: 2. Of those that a mesh axis runs over, the one named last changes fastest.
Arguments:
- hidden: bfloat16 [12288, 12288], P('dp', 'tensor'), may hold values from -6 to 6
- residual_in: bfloat16 [12288, 6144], P('dp', 'tensor'), may hold values from -6 to 6
- w_down: bfloat16 [12288, 6144], P('tensor', 'dp'), may hold values from -0.0546875 to 0.0546875
- w_key: bfloat16 [6144, 2048], P('tensor', 'dp'), may hold values from -0.078125 to 0.078125
- w_value: bfloat16 [6144, 2048], P('tensor', 'dp'), may hold values from -0.078125 to 0.078125
- queries: float32 [512, 2048], P('dp'), may hold values from -6 to 6
- w_query: bfloat16 [2048, 2048], P(None, 'tensor'), may hold values from -0.125 to 0.125
- attn_bias: float32 [16, 32, 768], P('dp'), as said below
- w_out: bfloat16 [2048, 2048], replicated, may hold values from -0.125 to 0.125
- w_in: bfloat16 [2048, 8192], P(None, 'tensor'), may hold values from -0.125 to 0.125
- w_back: bfloat16 [8192, 2048], P('tensor'), may hold values from -0.0625 to 0.0625
Outputs:
- query_out: bfloat16 [512, 2048], P('dp')
Inputs may be any that keep to these rules, and one draw needn't show every extreme that they name: `attn_bias`: the same bias for every head of an image.
All inputs are finite; a program needn't handle non-finite values.
Results may differ from a plain program's by a relative error of at most 0.024.
Values may be sent and summed in bfloat16 or wider, within the bound.
No kernel may reach another device: no remote copies, remote signals or barrier semaphores. Data moves between devices by JAX's collectives and lax.ppermute only.
A program may use at most 192 MiB of HBM per device.

v0:
```python
import jax
import jax.numpy as jnp
from jax import lax
from jax.sharding import PartitionSpec as P

HEAD_DIM = 128
AXES = ("dp", "tensor")
BF16 = jnp.bfloat16
F32 = jnp.float32


def layer_norm(x):
    mean = jnp.mean(x, axis=-1, keepdims=True)
    centered = x - mean
    var = jnp.mean(centered * centered, axis=-1, keepdims=True)
    return centered * lax.rsqrt(var + 1e-06)


def matmul(a, b):
    return jnp.dot(a, b, preferred_element_type=F32)


def matmul_t(a, b):
    return lax.dot_general(a, b, (((1,), (1,)), ((), ())), preferred_element_type=F32)


def doubling_blocks(x, arrived):
    got = x[None]
    for bit in range(3):
        if bit == 1:
            got, _ = lax.optimization_barrier((got, arrived))
        got = jnp.concatenate(
            [got, lax.ppermute(got, "tensor", [(s, s ^ (1 << bit)) for s in range(8)])], axis=0
        )
    return [got[j] for j in range(8)]


def shifts(move):
    pairs = []
    for s in range(128):
        d, t = s // 8, s % 8
        to = move(t // 4, d // 8, d // 2 % 4, t % 4, d % 2)
        if to is not None:
            xh, xl, y, z, c = to
            pairs.append((s, ((xl * 4 + y % 4) * 2 + c) * 8 + xh * 4 + z % 4))
    return pairs


def send(x, pairs):
    return lax.ppermute(x, AXES, pairs)


OTHER_CORE = shifts(lambda xh, xl, y, z, c: (xh, xl, y, z, 1 - c))
X_LO = shifts(lambda xh, xl, y, z, c: (xh, 1 - xl, y, z, c))
Y_UP = shifts(lambda xh, xl, y, z, c: (xh, xl, y + 1, z, c))
Y_DOWN = shifts(lambda xh, xl, y, z, c: (xh, xl, y + 3, z, c))
Z_UP = shifts(lambda xh, xl, y, z, c: (xh, xl, y, z + 1, c))
Z_DOWN = shifts(lambda xh, xl, y, z, c: (xh, xl, y, z + 3, c))
X_FIRST = shifts(lambda xh, xl, y, z, c: ((1, 0), (0, 0), (1, 1), (0, 1))[2 * xh + xl] + (y, z, c))
X_SECOND = shifts(lambda xh, xl, y, z, c: (1 - xh, 1 - xl, y, z, c) if xh != xl else None)


def ring_gather(x, up, down):
    half = x.shape[0] // 2
    below = send(x, up)
    above = send(x, down)
    far = [send(below[:half], up), send(above[half:], down)]
    return [x, above, jnp.concatenate(far, axis=0), below]


def in_order(blocks):
    me = lax.axis_index("tensor")
    stacked = jnp.stack(blocks)
    return jnp.stack(
        [lax.dynamic_index_in_dim(stacked, me ^ g, 0, keepdims=False) for g in range(8)]
    )


def tensor_sum(x):
    def from_xor(v, j):
        return lax.ppermute(v, "tensor", [(s, s ^ j) for s in range(8)]).astype(F32)

    x = (x.astype(F32) + from_xor(x, 4)).astype(BF16)
    return (x.astype(F32) + from_xor(x, 1)) + (from_xor(x, 2) + from_xor(x, 3))


def chip_gather(x):
    half = x.shape[0] // 2
    below, above, beside = send(x, Y_UP), send(x, Y_DOWN), send(x, X_LO)
    far = jnp.concatenate([send(below[:half], Y_UP), send(above[half:], Y_DOWN)], axis=0)
    beside_below, beside_above = send(beside, Y_UP), send(beside, Y_DOWN)
    beside_far = send(far, X_LO)
    return [x, above, far, below], [beside, beside_above, beside_far, beside_below]


def shards(
    hidden, residual_in, w_down, w_key, w_value, queries, w_query, attn_bias, w_out, w_in, w_back
):
    nq = queries.shape[0]
    ff = hidden.shape[1]
    e = HEAD_DIM
    d, t = lax.axis_index("dp"), lax.axis_index("tensor")
    core, y, x_lo = d % 2, d // 2 % 4, d // 8
    z, x_hi = t % 4, t // 4
    scale = 1.0 / HEAD_DIM**0.5
    down = ring_gather(w_down, Y_UP, Y_DOWN)
    rows = w_key.shape[0] // 2
    kv = jnp.concatenate([w_key, w_value], axis=1)
    mine = lax.dynamic_slice_in_dim(kv, core * rows, rows, 0)
    got = send(lax.dynamic_slice_in_dim(kv, (1 - core) * rows, rows, 0), OTHER_CORE)
    both = jnp.concatenate([mine[:, :e], got[:, :e], mine[:, e:], got[:, e:]], axis=1)
    first, second = send(both, X_FIRST), send(both, X_SECOND)
    inner_chip = x_hi == x_lo
    own = jnp.where(inner_chip, both, first)
    other = jnp.where(inner_chip, first, second)
    pieces = [a[:, i * e : (i + 1) * e] for i in range(4) for a in (own, other)]
    kv_rows = jnp.concatenate(pieces, axis=1)
    qnorm = layer_norm(queries).astype(BF16)
    qproj = (matmul(qnorm, w_query) * scale).astype(BF16)
    q_heads = in_order(doubling_blocks(qproj, (first, second)))
    q_heads = q_heads.reshape(8, nq, 2, e).transpose(0, 2, 1, 3).reshape(16 * nq, e)
    q_all = lax.all_to_all(q_heads, "dp", 0, 0, tiled=True)
    half = rows // 2
    below, above = send(kv_rows, Z_UP), send(kv_rows, Z_DOWN)
    (below, above), q_all = lax.optimization_barrier(((below, above), q_all))
    far = jnp.concatenate([send(below[:half], Z_UP), send(above[half:], Z_DOWN)], axis=0)
    kv_rows = jnp.stack([kv_rows, above, far, below])

    def product(blocks, stacked):
        total = None
        for r in range(4):
            weights = lax.dynamic_index_in_dim(stacked, (y + r - z) % 4, 0, keepdims=False)
            term = matmul(blocks[r], weights)
            total = term if total is None else total + term
        return total

    def core_sum(part):
        return part[:, : 2 * e] + send(part[:, 2 * e :].astype(BF16), OTHER_CORE).astype(F32)

    def x_sum(here):
        return (here[:, :e] + send(here[:, e:].astype(BF16), X_LO).astype(F32)).astype(BF16)

    cut = 4 * e
    key_rows, value_rows = kv_rows[:, :, :cut], kv_rows[:, :, cut:]
    key_sum = core_sum(product(down, key_rows))
    value_rows, key_sum = lax.optimization_barrier((value_rows, key_sum))
    key_head = jnp.concatenate([x_sum(key_sum), w_key], axis=0)
    value_head = jnp.concatenate([x_sum(core_sum(product(down, value_rows))), w_value], axis=0)
    wide = lax.all_to_all(matmul_t(q_all, key_head).astype(BF16), "dp", 0, 0, tiled=True)
    value_head, wide = lax.optimization_barrier((value_head, wide))
    near, beside = chip_gather(value_head)
    values = [jnp.stack(near), jnp.stack(beside)]
    values = values + [send(v, OTHER_CORE) for v in values]
    part = matmul_t(wide[:, :ff], hidden) + matmul_t(wide[:, ff:], residual_in)
    part = lax.all_to_all(part.astype(BF16), "tensor", 0, 0, tiled=True)
    scores = jnp.sum(part.reshape(8, 2, nq, -1).astype(F32), axis=0) + attn_bias[0][None]
    probs = jax.nn.softmax(scores, axis=-1).astype(BF16).reshape(1, 2 * nq, -1)
    probs = jnp.broadcast_to(probs, (8,) + probs.shape[1:]).reshape(16 * nq, -1)
    probs = lax.all_to_all(probs, "tensor", 0, 0, tiled=True)
    def head_of(k):
        return ((x_lo ^ (k // 4 % 2)) * 4 + (y + k) % 4) * 2 + (core ^ (k // 8))

    row = lax.broadcasted_iota(jnp.int32, (16 * nq, 16 * nq), 0)
    column = lax.broadcasted_iota(jnp.int32, (16 * nq, 16 * nq), 1)
    moves = (head_of(row // nq) * nq + row % nq == column).astype(BF16)
    probs = matmul(moves, probs).astype(BF16)
    wide = jnp.concatenate([matmul(probs, hidden), matmul(probs, residual_in)], axis=1)
    wide = wide.astype(BF16).reshape(4, 4, nq, -1)
    part = [
        lax.dot_general(wide[i], values[i], (((2,), (1,)), ((0,), (0,))), preferred_element_type=F32)
        for i in range(4)
    ]
    part = jnp.concatenate(part, axis=0).astype(BF16)
    places = [
        (core ^ (h % 2)) * 8 + (x_lo ^ (h // 8)) * 4 + (h // 2 - y) % 4 for h in range(16)
    ]
    part = jnp.concatenate(
        [lax.dynamic_index_in_dim(part, k, 0, keepdims=False) for k in places], axis=1
    )
    attended = tensor_sum(part).astype(BF16)
    mid = queries + matmul(attended, w_out)
    mnorm = layer_norm(mid).astype(BF16)
    inner = jax.nn.gelu(matmul(mnorm, w_in)).astype(BF16)
    back = tensor_sum(matmul(inner, w_back).astype(BF16))
    return (mid + back).astype(BF16)


def solution(mesh):
    in_specs = (
        P("dp", "tensor"),
        P("dp", "tensor"),
        P("tensor", "dp"),
        P("tensor", "dp"),
        P("tensor", "dp"),
        P("dp", None),
        P(None, "tensor"),
        P("dp", None, None),
        P(),
        P(None, "tensor"),
        P("tensor", None),
    )
    out_specs = P("dp", None)
    return jax.shard_map(shards, mesh=mesh, in_specs=in_specs, out_specs=out_specs, check_vma=False)
```

profile of v0, /device:TPU:0, one launch (start us, length us, event | category | flops | bytes accessed | tf_op | source)
XLA Modules:
  0.0 266.5 jit_solution(4954131548692283998)
XLA Ops:
  6.9 4.2 %collective-permute-start.1 = (bf16[384,512]{1,0:T(8,128)(2,1)}, bf16[384,512]{1,0:T(8,128)(2,1)}, u32[]{:S(2)}, u32[]{:S(2)}) collective-permute-start(bf16[384,512]{1,0:T(8,128)(2,1)} %pad_maximum_fusion.5), channel_id=1, source_target_pairs={{0,4},{1,5},{2,6},{3,7},{4,68},{5,69},{6,70},{7,71},{8,12},{9,13},... | collective-permute-start | bytes 1179656 | tf_op jit(solution)/shard_map/ppermute | solution.py:50
  12.6 2.0 collective-permute-start.5
  14.6 3.0 %collective-permute-start.10 = (bf16[1536,384]{1,0:T(8,128)(2,1)}, bf16[1536,384]{1,0:T(8,128)(2,1)}, u32[]{:S(2)}, u32[]{:S(2)}) collective-permute-start(bf16[1536,384]{1,0:T(8,128)(2,1)} %param.13), channel_id=1, source_target_pairs={{0,48},{1,49},{2,50},{3,51},{4,52},{5,53},{6,54},{7,55},{8,56},{9,... | collective-permute-start | bytes 3538952 | tf_op jit(solution)/shard_map/ppermute | solution.py:50
  18.6 1.7 collective-permute-done.1
  20.3 3.9 %collective-permute-start.6 = (bf16[2,32,256]{2,1,0:T(8,128)(2,1)S(1)}, bf16[2,32,256]{2,1,0:T(8,128)(2,1)S(1)}, u32[]{:S(2)}, u32[]{:S(2)}) collective-permute-start(bf16[2,32,256]{2,1,0:T(8,128)(2,1)S(1)} %pad_maximum_fusion.9), channel_id=1, source_target_pairs={{0,2},{1,3},{2,0},{3,1},{4,6},{5,7},{6,4},{7,5},{8,10},{9,11},{10,... | collective-permute-start | bytes 98312 | tf_op jit(solution)/shard_map/ppermute | solution.py:33
  27.9 10.6 %collective-permute-start.7 = (bf16[4,32,256]{2,1,0:T(8,128)(2,1)S(1)}, bf16[4,32,256]{2,1,0:T(8,128)(2,1)S(1)}, u32[]{:S(2)}, u32[]{:S(2)}) collective-permute-start(bf16[4,32,256]{2,1,0:T(8,128)(2,1)S(1)} %pad_maximum_fusion.8), channel_id=1, source_target_pairs={{0,4},{1,5},{2,6},{3,7},{4,0},{5,1},{6,2},{7,3},{8,12},{9,13},{10,... | collective-permute-start | bytes 196616 | tf_op jit(solution)/shard_map/ppermute | solution.py:33
  38.5 2.2 collective-permute-done.7
  40.9 12.6 %all_to_all.42 = bf16[16,32,128]{2,1,0:T(8,128)(2,1)} all-to-all(bf16[16,32,128]{2,1,0:T(8,128)(2,1)S(1)} %bitcast.176), channel_id=1, replica_groups=mesh['dp'=16,'tensor'=8] {'dp'}, dimensions={0} | all-to-all | bytes 262144 | tf_op jit(solution)/shard_map/all_to_all | solution.py:122
  57.0 2.2 collective-permute-start.9
  62.8 5.6 %collective-permute-done.8 = bf16[192,1024]{1,0:T(8,128)(2,1)} collective-permute-done((bf16[192,1024]{1,0:T(8,128)(2,1)}, bf16[192,1024]{1,0:T(8,128)(2,1)}, u32[]{:S(2)}, u32[]{:S(2)}) %collective-permute-start.8) | collective-permute-done | bytes 393248 | tf_op jit(solution)/shard_map/ppermute | solution.py:50
  71.4 6.1 %collective-permute-done.12 = bf16[768,384]{1,0:T(8,128)(2,1)S(1)} collective-permute-done((bf16[768,384]{1,0:T(8,128)(2,1)S(1)}, bf16[768,384]{1,0:T(8,128)(2,1)S(1)}, u32[]{:S(2)}, u32[]{:S(2)}) %collective-permute-start.12) | collective-permute-done | bytes 589856 | tf_op jit(solution)/shard_map/ppermute | solution.py:50
  77.6 2.3 fusion.69
  81.1 2.8 %fusion.2 = f32[1536,512]{0,1:T(8,128)S(1)} fusion(f32[512,1536]{1,0:T(8,128)S(1)} %fusion.69, bf16[1536,384]{1,0:T(8,128)(2,1)} %collective-permute-done.10, bf16[4,384,512]{2,1,0:T(8,128)(2,1)S(1)} %get-tuple-element.21, s32[]{:T(128)S(6)} %select_n.263), kind=kOutput, calls=%fused_computation.10 | convolution fusion | flops 604766208 | bytes 7864324 | tf_op jit(solution)/shard_map/dot_general | solution.py:20
  87.7 1.7 copy.23
  90.3 1.8 slice_add_fusion.1
  93.6 2.3 fusion.64
  97.0 2.4 fusion.3
  100.7 2.9 %collective-permute-done.17 = bf16[1536,128]{0,1:T(8,128)(2,1)S(1)} collective-permute-done((bf16[1536,128]{0,1:T(8,128)(2,1)S(1)}, bf16[1536,128]{0,1:T(8,128)(2,1)S(1)}, u32[]{:S(2)}, u32[]{:S(2)}) %collective-permute-start.17) | collective-permute-done | bytes 393248 | tf_op jit(solution)/shard_map/ppermute | solution.py:50
  103.7 2.2 convolution_convert_fusion
  105.9 4.4 %all-to-all-start.1 = ((bf16[16,32,2304]{2,1,0:T(8,128)(2,1)}), bf16[16,32,2304]{2,1,0:T(8,128)(2,1)}, u32[]{:S(2)}, u32[]{:S(2)}) async-start(bf16[16,32,2304]{2,1,0:T(8,128)(2,1)} %bitcast.162), calls=%async_computation.1 | async-start | bytes 4718592 | tf_op jit(solution)/shard_map/all_to_all | solution.py:149
  110.4 1.8 slice_add_fusion
  113.4 1.9 collective-permute-start.16
  115.5 33.6 %collective-permute-done.16 = bf16[1536,128]{0,1:T(8,128)(2,1)} collective-permute-done((bf16[1536,128]{0,1:T(8,128)(2,1)S(1)}, bf16[1536,128]{0,1:T(8,128)(2,1)}, u32[]{:S(2)}, u32[]{:S(2)}) %collective-permute-start.16) | collective-permute-done | bytes 393248 | tf_op jit(solution)/shard_map/ppermute | solution.py:50
  151.2 4.6 %collective-permute-start.19 = (bf16[2304,128]{0,1:T(8,128)(2,1)}, bf16[2304,128]{0,1:T(8,128)(2,1)S(1)}, u32[]{:S(2)}, u32[]{:S(2)}) collective-permute-start(bf16[2304,128]{0,1:T(8,128)(2,1)} %pad_maximum_fusion.4), channel_id=1, source_target_pairs={{0,16},{1,17},{2,18},{3,19},{4,20},{5,21},{6,22},{7,23},{8,24},{9,... | collective-permute-start | bytes 1769480 | tf_op jit(solution)/shard_map/ppermute | solution.py:50
  156.3 2.8 %fusion.7 = f32[512,768]{1,0:T(8,128)S(1)} fusion(bf16[768,1536]{1,0:T(8,128)(2,1)S(1)} %copy-done, bf16[512,2304]{1,0:T(8,128)(2,1)} %bitcast.20), kind=kOutput, calls=%fused_computation.37 | convolution fusion | flops 1207959552 | bytes 5505024 | tf_op jit(solution)/shard_map/dot_general | solution.py:24
  159.2 9.4 %collective-permute-done.19 = bf16[2304,128]{0,1:T(8,128)(2,1)S(1)} collective-permute-done((bf16[2304,128]{0,1:T(8,128)(2,1)}, bf16[2304,128]{0,1:T(8,128)(2,1)S(1)}, u32[]{:S(2)}, u32[]{:S(2)}) %collective-permute-start.19) | collective-permute-done | bytes 589856 | tf_op jit(solution)/shard_map/ppermute | solution.py:50
  169.3 2.4 collective-permute-start.20
  171.7 2.9 %add_convert_fusion = bf16[512,768]{1,0:T(8,128)(2,1)} fusion(f32[512,768]{1,0:T(8,128)S(1)} %fusion.7, bf16[768,768]{1,0:T(8,128)(2,1)S(1)} %copy-done.25, bf16[512,2304]{1,0:T(8,128)(2,1)} %bitcast.20), kind=kOutput, calls=%fused_computation.36 | convolution fusion | flops 604766208 | bytes 4325376 | tf_op jit(solution)/shard_map/dot_general | solution.py:24
  174.6 4.1 %all-to-all-start.2 = ((bf16[8,64,768]{2,1,0:T(8,128)(2,1)}), bf16[8,64,768]{2,1,0:T(8,128)(2,1)S(1)}, u32[]{:S(2)}, u32[]{:S(2)}) async-start(bf16[8,64,768]{2,1,0:T(8,128)(2,1)} %bitcast.174), calls=%async_computation.2 | async-start | bytes 1572864 | tf_op jit(solution)/shard_map/all_to_all | solution.py:155
  181.8 2.1 collective-permute-start.23
  184.6 5.1 %collective-permute-done.21 = bf16[1152,128]{0,1:T(8,128)(2,1)S(1)} collective-permute-done((bf16[1152,128]{0,1:T(8,128)(2,1)S(1)}, bf16[1152,128]{0,1:T(8,128)(2,1)S(1)}, u32[]{:S(2)}, u32[]{:S(2)}) %collective-permute-start.21) | collective-permute-done | bytes 294944 | tf_op jit(solution)/shard_map/ppermute | solution.py:50
  192.6 7.2 %all-to-all-start.3 = ((bf16[8,64,768]{2,1,0:T(8,128)(2,1)}), bf16[8,64,768]{2,1,0:T(8,128)(2,1)}, u32[]{:S(2)}, u32[]{:S(2)}) async-start(bf16[8,64,768]{2,1,0:T(8,128)(2,1)} %broadcast_in_dim.5), calls=%async_computation.3 | async-start | bytes 1572864 | tf_op jit(solution)/shard_map/all_to_all | solution.py:159
  199.8 3.1 %pad_maximum_fusion.1 = bf16[4,2304,128]{1,2,0:T(8,128)(2,1)} fusion(bf16[1,2304,128]{1,2,0:T(8,128)(2,1)S(1)} %bitcast.169, bf16[1,2304,128]{1,2,0:T(8,128)(2,1)} %bitcast.28, bf16[1,2304,128]{1,2,0:T(8,128)(2,1)} %bitcast.27, bf16[1,2304,128]{1,2,0:T(8,128)(2,1)} %bitcast.26), kind=kLoop, calls=%fused_computation.24 | loop fusion | flops 3538944 | bytes 4718592 | tf_op jit(solution)/shard_map/stack | solution.py:152
  204.2 3.3 %pad_maximum_fusion.2 = bf16[4,2304,128]{1,2,0:T(8,128)(2,1)} fusion(bf16[1,2304,128]{1,2,0:T(8,128)(2,1)} %bitcast.34, bf16[1,2304,128]{1,2,0:T(8,128)(2,1)} %bitcast.33, bf16[1,2304,128]{1,2,0:T(8,128)(2,1)} %bitcast.32, bf16[1,2304,128]{1,2,0:T(8,128)(2,1)} %bitcast.31), kind=kLoop, calls=%fused_computation.25 | loop fusion | flops 3538944 | bytes 4718592 | tf_op jit(solution)/shard_map/stack | solution.py:152
  207.5 5.0 %all-to-all-done.3 = bf16[8,64,768]{2,1,0:T(8,128)(2,1)} async-done(((bf16[8,64,768]{2,1,0:T(8,128)(2,1)}), bf16[8,64,768]{2,1,0:T(8,128)(2,1)}, u32[]{:S(2)}, u32[]{:S(2)}) %all-to-all-start.3) | async-done | bytes 786464 | tf_op jit(solution)/shard_map/all_to_all | solution.py:159
  212.5 2.9 %convolution_convert_fusion.4 = bf16[512,768]{1,0:T(8,128)(2,1)S(1)} fusion(bf16[512,768]{1,0:T(8,128)(2,1)} %bitcast.24, s32[512]{0:T(512)S(1)} %get-tuple-element.40, s32[512]{0:T(512)S(1)} %get-tuple-element.41, s32[]{:T(128)S(6)} %select_n.242, s32[]{:T(128)S(6)} %select_n.240, s32[512]{0:T(512)S(1)} %get-tuple-element.39, ...), kind=kOutput, calls=%fused_computation.51 | convolution fusion | flops 418512896 | bytes 1582092 | tf_op jit(solution)/shard_map/dot_general | solution.py:20
  217.8 2.7 convolution_convert_fusion.8
  220.4 2.7 convolution_convert_fusion.7
  223.1 2.5 convolution_convert_fusion.6
  225.7 2.6 convolution_convert_fusion.5
  229.0 6.2 %collective-permute-done.28 = bf16[32,2048]{1,0:T(8,128)(2,1)S(1)} collective-permute-done((bf16[32,2048]{1,0:T(8,128)(2,1)S(1)}, bf16[32,2048]{1,0:T(8,128)(2,1)S(1)}, u32[]{:S(2)}, u32[]{:S(2)}) %collective-permute-start.28) | collective-permute-done | bytes 131104 | tf_op jit(solution)/shard_map/ppermute | solution.py:81
  237.5 1.9 collective-permute-start.29
  239.4 2.1 collective-permute-done.31
  241.4 1.6 collective-permute-done.30
  243.7 1.6 fusion.146
  245.6 5.1 %convolution_convert_fusion.2 = bf16[32,2048]{1,0:T(8,128)(2,1)S(1)} fusion(bf16[1024,2048]{1,0:T(8,128)(2,1)} %param.21, bf16[2048,1024]{1,0:T(8,128)(2,1)} %param.20, f32[32,2048]{1,0:T(8,128)S(1)} %get-tuple-element.36, f32[32]{0:T(128)S(1)} %add_rsqrt_fusion, f32[32]{0:T(128)S(1)} %broadcast_multiply_fusion), kind=kOutput, calls=%fused_computation.27 | convolution fusion | flops 268992512 | bytes 8782080 | tf_op jit(solution)/shard_map/dot_general | solution.py:20
  251.1 6.1 %collective-permute-done.32 = bf16[32,2048]{1,0:T(8,128)(2,1)S(1)} collective-permute-done((bf16[32,2048]{1,0:T(8,128)(2,1)S(1)}, bf16[32,2048]{1,0:T(8,128)(2,1)S(1)}, u32[]{:S(2)}, u32[]{:S(2)}) %collective-permute-start.32) | collective-permute-done | bytes 131104 | tf_op jit(solution)/shard_map/ppermute | solution.py:81
  261.5 2.1 collective-permute-done.35
  (203 shorter events, 59.1 us)
Async XLA Ops:
  0.0 156.3 %copy-start = (bf16[768,1536]{1,0:T(8,128)(2,1)S(1)}, bf16[768,1536]{1,0:T(8,128)(2,1)}, u32[]{:S(2)}) copy-start(bf16[768,1536]{1,0:T(8,128)(2,1)} %param.11) | copy-start | bytes 7077892
  2.1 2.5 collective-permute-start
  3.4 14.3 %copy-start.18 = (bf16[384,128]{1,0:T(8,128)(2,1)}, bf16[384,128]{1,0:T(8,128)(2,1)S(1)}, u32[]{:S(2)}) copy-start(bf16[384,128]{1,0:T(8,128)(2,1)S(1)} %get-tuple-element.30) | copy-start | bytes 294916
  4.6 13.0 %copy-start.19 = (bf16[384,128]{1,0:T(8,128)(2,1)}, bf16[384,128]{1,0:T(8,128)(2,1)S(1)}, u32[]{:S(2)}) copy-start(bf16[384,128]{1,0:T(8,128)(2,1)S(1)} %get-tuple-element.31) | copy-start | bytes 294916
  5.5 13.1 %collective-permute-start.2 = (bf16[384,512]{1,0:T(8,128)(2,1)}, bf16[384,512]{1,0:T(8,128)(2,1)}, u32[]{:S(2)}, u32[]{:S(2)}) collective-permute-start(bf16[384,512]{1,0:T(8,128)(2,1)} %pad_maximum_fusion.5), channel_id=1, source_target_pairs={{4,64},{5,65},{6,66},{7,67},{12,72},{13,73},{14,74},{15,75},{20,80... | collective-permute-start | bytes 1179656 | tf_op jit(solution)/shard_map/ppermute | solution.py:50
  6.9 13.4 %collective-permute-start.1 = (bf16[384,512]{1,0:T(8,128)(2,1)}, bf16[384,512]{1,0:T(8,128)(2,1)}, u32[]{:S(2)}, u32[]{:S(2)}) collective-permute-start(bf16[384,512]{1,0:T(8,128)(2,1)} %pad_maximum_fusion.5), channel_id=1, source_target_pairs={{0,4},{1,5},{2,6},{3,7},{4,68},{5,69},{6,70},{7,71},{8,12},{9,13},... | collective-permute-start | bytes 1179656 | tf_op jit(solution)/shard_map/ppermute | solution.py:50
  12.6 5.2 %collective-permute-start.5 = (bf16[1,32,256]{2,1,0:T(8,128)(2,1)S(1)}, bf16[1,32,256]{2,1,0:T(8,128)(2,1)}, u32[]{:S(2)}, u32[]{:S(2)}) collective-permute-start(bf16[1,32,256]{2,1,0:T(8,128)(2,1)S(1)} %fusion.10), channel_id=1, source_target_pairs={{0,1},{1,0},{2,3},{3,2},{4,5},{5,4},{6,7},{7,6},{8,9},{9,8},{10,11... | collective-permute-start | bytes 49160 | tf_op jit(solution)/shard_map/ppermute | solution.py:33
  14.6 44.6 %collective-permute-start.10 = (bf16[1536,384]{1,0:T(8,128)(2,1)}, bf16[1536,384]{1,0:T(8,128)(2,1)}, u32[]{:S(2)}, u32[]{:S(2)}) collective-permute-start(bf16[1536,384]{1,0:T(8,128)(2,1)} %param.13), channel_id=1, source_target_pairs={{0,48},{1,49},{2,50},{3,51},{4,52},{5,53},{6,54},{7,55},{8,56},{9,... | collective-permute-start | bytes 3538952 | tf_op jit(solution)/shard_map/ppermute | solution.py:50
  17.7 44.0 %collective-permute-start.11 = (bf16[1536,384]{1,0:T(8,128)(2,1)}, bf16[1536,384]{1,0:T(8,128)(2,1)S(1)}, u32[]{:S(2)}, u32[]{:S(2)}) collective-permute-start(bf16[1536,384]{1,0:T(8,128)(2,1)} %param.13), channel_id=1, source_target_pairs={{0,16},{1,17},{2,18},{3,19},{4,20},{5,21},{6,22},{7,23},{8,24},{9,... | collective-permute-start | bytes 3538952 | tf_op jit(solution)/shard_map/ppermute | solution.py:50
  20.3 7.6 %collective-permute-start.6 = (bf16[2,32,256]{2,1,0:T(8,128)(2,1)S(1)}, bf16[2,32,256]{2,1,0:T(8,128)(2,1)S(1)}, u32[]{:S(2)}, u32[]{:S(2)}) collective-permute-start(bf16[2,32,256]{2,1,0:T(8,128)(2,1)S(1)} %pad_maximum_fusion.9), channel_id=1, source_target_pairs={{0,2},{1,3},{2,0},{3,1},{4,6},{5,7},{6,4},{7,5},{8,10},{9,11},{10,... | collective-permute-start | bytes 98312 | tf_op jit(solution)/shard_map/ppermute | solution.py:33
  25.8 27.8 %copy-start.15 = (bf16[384,1024]{1,0:T(8,128)(2,1)}, bf16[384,1024]{1,0:T(8,128)(2,1)S(1)}, u32[]{:S(2)}) copy-start(bf16[384,1024]{1,0:T(8,128)(2,1)S(1)} %slice_dynamic-update-slice_fusion) | copy-start | bytes 2359300
  25.8 27.7 %collective-permute-start.4 = (bf16[384,1024]{1,0:T(8,128)(2,1)S(1)}, bf16[384,1024]{1,0:T(8,128)(2,1)S(1)}, u32[]{:S(2)}, u32[]{:S(2)}) collective-permute-start(bf16[384,1024]{1,0:T(8,128)(2,1)S(1)} %slice_dynamic-update-slice_fusion), channel_id=1, source_target_pairs={{0,3},{1,0},{2,1},{3,2},{4,7},{5,4},{6,5},{7,6},{8,11},{9,8},{10,9... | collective-permute-start | bytes 2359304 | tf_op jit(solution)/shard_map/ppermute | solution.py:50
  26.6 26.9 %collective-permute-start.3 = (bf16[384,1024]{1,0:T(8,128)(2,1)S(1)}, bf16[384,1024]{1,0:T(8,128)(2,1)S(1)}, u32[]{:S(2)}, u32[]{:S(2)}) collective-permute-start(bf16[384,1024]{1,0:T(8,128)(2,1)S(1)} %slice_dynamic-update-slice_fusion), channel_id=1, source_target_pairs={{0,1},{1,2},{2,3},{3,0},{4,5},{5,6},{6,7},{7,4},{8,9},{9,10},{10,1... | collective-permute-start | bytes 2359304 | tf_op jit(solution)/shard_map/ppermute | solution.py:50
  27.9 12.8 %collective-permute-start.7 = (bf16[4,32,256]{2,1,0:T(8,128)(2,1)S(1)}, bf16[4,32,256]{2,1,0:T(8,128)(2,1)S(1)}, u32[]{:S(2)}, u32[]{:S(2)}) collective-permute-start(bf16[4,32,256]{2,1,0:T(8,128)(2,1)S(1)} %pad_maximum_fusion.8), channel_id=1, source_target_pairs={{0,4},{1,5},{2,6},{3,7},{4,0},{5,1},{6,2},{7,3},{8,12},{9,13},{10,... | collective-permute-start | bytes 196616 | tf_op jit(solution)/shard_map/ppermute | solution.py:33
  56.0 12.4 %collective-permute-start.8 = (bf16[192,1024]{1,0:T(8,128)(2,1)}, bf16[192,1024]{1,0:T(8,128)(2,1)}, u32[]{:S(2)}, u32[]{:S(2)}) collective-permute-start(bf16[192,1024]{1,0:T(8,128)(2,1)} %slice.141), channel_id=1, source_target_pairs={{0,1},{1,2},{2,3},{3,0},{4,5},{5,6},{6,7},{7,4},{8,9},{9,10},{10,1... | collective-permute-start | bytes 1179656 | tf_op jit(solution)/shard_map/ppermute | solution.py:50
  57.0 11.4 %collective-permute-start.9 = (bf16[192,1024]{1,0:T(8,128)(2,1)}, bf16[192,1024]{1,0:T(8,128)(2,1)}, u32[]{:S(2)}, u32[]{:S(2)}) collective-permute-start(bf16[192,1024]{1,0:T(8,128)(2,1)} %slice.142), channel_id=1, source_target_pairs={{0,3},{1,0},{2,1},{3,2},{4,7},{5,4},{6,5},{7,6},{8,11},{9,8},{10,9... | collective-permute-start | bytes 1179656 | tf_op jit(solution)/shard_map/ppermute | solution.py:50
  60.5 20.5 %collective-permute-start.13 = (bf16[768,384]{1,0:T(8,128)(2,1)S(1)}, bf16[768,384]{1,0:T(8,128)(2,1)S(1)}, u32[]{:S(2)}, u32[]{:S(2)}) collective-permute-start(bf16[768,384]{1,0:T(8,128)(2,1)S(1)} %slice.178), channel_id=1, source_target_pairs={{0,48},{1,49},{2,50},{3,51},{4,52},{5,53},{6,54},{7,55},{8,56},{9,... | collective-permute-start | bytes 1769480 | tf_op jit(solution)/shard_map/ppermute | solution.py:50
  61.7 15.8 %collective-permute-start.12 = (bf16[768,384]{1,0:T(8,128)(2,1)S(1)}, bf16[768,384]{1,0:T(8,128)(2,1)S(1)}, u32[]{:S(2)}, u32[]{:S(2)}) collective-permute-start(bf16[768,384]{1,0:T(8,128)(2,1)S(1)} %slice.177), channel_id=1, source_target_pairs={{0,16},{1,17},{2,18},{3,19},{4,20},{5,21},{6,22},{7,23},{8,24},{9,... | collective-permute-start | bytes 1769480 | tf_op jit(solution)/shard_map/ppermute | solution.py:50
  87.7 2.6 collective-permute-start.14
  92.1 11.4 %collective-permute-start.17 = (bf16[1536,128]{0,1:T(8,128)(2,1)S(1)}, bf16[1536,128]{0,1:T(8,128)(2,1)S(1)}, u32[]{:S(2)}, u32[]{:S(2)}) collective-permute-start(bf16[1536,128]{0,1:T(8,128)(2,1)S(1)} %slice.236), channel_id=1, source_target_pairs={{0,64},{1,65},{2,66},{3,67},{4,68},{5,69},{6,70},{7,71},{8,72},{9,... | collective-permute-start | bytes 1179656 | tf_op jit(solution)/shard_map/ppermute | solution.py:50
  100.6 9.8 %collective-permute-start.15 = (bf16[1536,256]{0,1:T(8,128)(2,1)S(1)}, bf16[1536,256]{0,1:T(8,128)(2,1)}, u32[]{:S(2)}, u32[]{:S(2)}) collective-permute-start(bf16[1536,256]{0,1:T(8,128)(2,1)S(1)} %slice.234), channel_id=1, source_target_pairs={{0,8},{1,9},{2,10},{3,11},{4,12},{5,13},{6,14},{7,15},{8,0},{9,1},... | collective-permute-start | bytes 2359304 | tf_op jit(solution)/shard_map/ppermute | solution.py:50
  105.9 45.3 %all-to-all-start.1 = ((bf16[16,32,2304]{2,1,0:T(8,128)(2,1)}), bf16[16,32,2304]{2,1,0:T(8,128)(2,1)}, u32[]{:S(2)}, u32[]{:S(2)}) async-start(bf16[16,32,2304]{2,1,0:T(8,128)(2,1)} %bitcast.162), calls=%async_computation.1 | async-start | bytes 4718592 | tf_op jit(solution)/shard_map/all_to_all | solution.py:149
  113.4 35.6 %collective-permute-start.16 = (bf16[1536,128]{0,1:T(8,128)(2,1)S(1)}, bf16[1536,128]{0,1:T(8,128)(2,1)}, u32[]{:S(2)}, u32[]{:S(2)}) collective-permute-start(bf16[1536,128]{0,1:T(8,128)(2,1)S(1)} %slice.237), channel_id=1, source_target_pairs={{0,64},{1,65},{2,66},{3,67},{4,68},{5,69},{6,70},{7,71},{8,72},{9,... | collective-permute-start | bytes 1179656 | tf_op jit(solution)/shard_map/ppermute | solution.py:50
  151.2 17.3 %collective-permute-start.19 = (bf16[2304,128]{0,1:T(8,128)(2,1)}, bf16[2304,128]{0,1:T(8,128)(2,1)S(1)}, u32[]{:S(2)}, u32[]{:S(2)}) collective-permute-start(bf16[2304,128]{0,1:T(8,128)(2,1)} %pad_maximum_fusion.4), channel_id=1, source_target_pairs={{0,16},{1,17},{2,18},{3,19},{4,20},{5,21},{6,22},{7,23},{8,24},{9,... | collective-permute-start | bytes 1769480 | tf_op jit(solution)/shard_map/ppermute | solution.py:50
  155.8 15.9 %copy-start.25 = (bf16[768,768]{1,0:T(8,128)(2,1)S(1)}, bf16[768,768]{1,0:T(8,128)(2,1)}, u32[]{:S(2)}) copy-start(bf16[768,768]{1,0:T(8,128)(2,1)} %param.12) | copy-start | bytes 3538948
  155.8 24.8 %collective-permute-start.22 = (bf16[2304,128]{0,1:T(8,128)(2,1)}, bf16[2304,128]{0,1:T(8,128)(2,1)}, u32[]{:S(2)}, u32[]{:S(2)}) collective-permute-start(bf16[2304,128]{0,1:T(8,128)(2,1)} %pad_maximum_fusion.4), channel_id=1, source_target_pairs={{0,64},{1,65},{2,66},{3,67},{4,68},{5,69},{6,70},{7,71},{8,72},{9,... | collective-permute-start | bytes 1769480 | tf_op jit(solution)/shard_map/ppermute | solution.py:50
  156.3 22.4 %collective-permute-start.18 = (bf16[2304,128]{0,1:T(8,128)(2,1)}, bf16[2304,128]{0,1:T(8,128)(2,1)}, u32[]{:S(2)}, u32[]{:S(2)}) collective-permute-start(bf16[2304,128]{0,1:T(8,128)(2,1)} %pad_maximum_fusion.4), channel_id=1, source_target_pairs={{0,48},{1,49},{2,50},{3,51},{4,52},{5,53},{6,54},{7,55},{8,56},{9,... | collective-permute-start | bytes 1769480 | tf_op jit(solution)/shard_map/ppermute | solution.py:50
  169.3 14.6 %collective-permute-start.20 = (bf16[1152,128]{0,1:T(8,128)(2,1)}, bf16[1152,128]{0,1:T(8,128)(2,1)S(1)}, u32[]{:S(2)}, u32[]{:S(2)}) collective-permute-start(bf16[1152,128]{0,1:T(8,128)(2,1)} %slice.188), channel_id=1, source_target_pairs={{0,16},{1,17},{2,18},{3,19},{4,20},{5,21},{6,22},{7,23},{8,24},{9,... | collective-permute-start | bytes 884744 | tf_op jit(solution)/shard_map/ppermute | solution.py:50
  174.6 16.6 %copy-start.21 = (f32[1,32,768]{2,1,0:T(8,128)S(1)}, f32[1,32,768]{2,1,0:T(8,128)}, u32[]{:S(2)}) copy-start(f32[1,32,768]{2,1,0:T(8,128)} %param.18) | copy-start | bytes 294916
  174.6 16.5 %all-to-all-start.2 = ((bf16[8,64,768]{2,1,0:T(8,128)(2,1)}), bf16[8,64,768]{2,1,0:T(8,128)(2,1)S(1)}, u32[]{:S(2)}, u32[]{:S(2)}) async-start(bf16[8,64,768]{2,1,0:T(8,128)(2,1)} %bitcast.174), calls=%async_computation.2 | async-start | bytes 1572864 | tf_op jit(solution)/shard_map/all_to_all | solution.py:155
  179.7 10.0 %collective-permute-start.21 = (bf16[1152,128]{0,1:T(8,128)(2,1)S(1)}, bf16[1152,128]{0,1:T(8,128)(2,1)S(1)}, u32[]{:S(2)}, u32[]{:S(2)}) collective-permute-start(bf16[1152,128]{0,1:T(8,128)(2,1)S(1)} %slice.189), channel_id=1, source_target_pairs={{0,48},{1,49},{2,50},{3,51},{4,52},{5,53},{6,54},{7,55},{8,56},{9,... | collective-permute-start | bytes 884744 | tf_op jit(solution)/shard_map/ppermute | solution.py:50
  180.6 22.3 %collective-permute-start.25 = (bf16[2304,128]{0,1:T(8,128)(2,1)}, bf16[2304,128]{0,1:T(8,128)(2,1)}, u32[]{:S(2)}, u32[]{:S(2)}) collective-permute-start(bf16[2304,128]{0,1:T(8,128)(2,1)} %collective-permute-done.22), channel_id=1, source_target_pairs={{0,16},{1,17},{2,18},{3,19},{4,20},{5,21},{6,22},{7,23},{8,24},{9,... | collective-permute-start | bytes 1769480 | tf_op jit(solution)/shard_map/ppermute | solution.py:50
  181.8 21.1 %collective-permute-start.23 = (bf16[2304,128]{0,1:T(8,128)(2,1)}, bf16[2304,128]{0,1:T(8,128)(2,1)}, u32[]{:S(2)}, u32[]{:S(2)}) collective-permute-start(bf16[2304,128]{0,1:T(8,128)(2,1)} %collective-permute-done.22), channel_id=1, source_target_pairs={{0,48},{1,49},{2,50},{3,51},{4,52},{5,53},{6,54},{7,55},{8,56},{9,... | collective-permute-start | bytes 1769480 | tf_op jit(solution)/shard_map/ppermute | solution.py:50
  190.4 13.8 %collective-permute-start.24 = (bf16[2304,128]{0,1:T(8,128)(2,1)}, bf16[2304,128]{0,1:T(8,128)(2,1)}, u32[]{:S(2)}, u32[]{:S(2)}) collective-permute-start(bf16[2304,128]{0,1:T(8,128)(2,1)} %constant_dynamic-update-slice_fusion.15), channel_id=1, source_target_pairs={{0,64},{1,65},{2,66},{3,67},{4,68},{5,69},{6,70},{7,71},{8,72},{9,... | collective-permute-start | bytes 1769480 | tf_op jit(solution)/shard_map/ppermute | solution.py:50
  192.6 20.0 %all-to-all-start.3 = ((bf16[8,64,768]{2,1,0:T(8,128)(2,1)}), bf16[8,64,768]{2,1,0:T(8,128)(2,1)}, u32[]{:S(2)}, u32[]{:S(2)}) async-start(bf16[8,64,768]{2,1,0:T(8,128)(2,1)} %broadcast_in_dim.5), calls=%async_computation.3 | async-start | bytes 1572864 | tf_op jit(solution)/shard_map/all_to_all | solution.py:159
  202.9 20.2 %collective-permute-start.26 = (bf16[4,2304,128]{1,2,0:T(8,128)(2,1)}, bf16[4,2304,128]{1,2,0:T(8,128)(2,1)}, u32[]{:S(2)}, u32[]{:S(2)}) collective-permute-start(bf16[4,2304,128]{1,2,0:T(8,128)(2,1)} %pad_maximum_fusion.1), channel_id=1, source_target_pairs={{0,8},{1,9},{2,10},{3,11},{4,12},{5,13},{6,14},{7,15},{8,0},{9,1},... | collective-permute-start | bytes 7077896 | tf_op jit(solution)/shard_map/ppermute | solution.py:50
  207.5 18.2 %collective-permute-start.27 = (bf16[4,2304,128]{1,2,0:T(8,128)(2,1)}, bf16[4,2304,128]{1,2,0:T(8,128)(2,1)}, u32[]{:S(2)}, u32[]{:S(2)}) collective-permute-start(bf16[4,2304,128]{1,2,0:T(8,128)(2,1)} %pad_maximum_fusion.2), channel_id=1, source_target_pairs={{0,8},{1,9},{2,10},{3,11},{4,12},{5,13},{6,14},{7,15},{8,0},{9,1},... | collective-permute-start | bytes 7077896 | tf_op jit(solution)/shard_map/ppermute | solution.py:50
  217.6 26.1 %slice-start = ((s8[8388608]{0:T(1024)(128)(4,1)}), s8[4194304]{0:T(1024)(128)(4,1)S(1)}, s32[]{:S(2)}) async-start(s8[8388608]{0:T(1024)(128)(4,1)} %bitcast.160), calls=%async_computation.4 | async-start | bytes 8388608
  220.4 23.3 %slice-start.1 = ((s8[8388608]{0:T(1024)(128)(4,1)}), s8[4194304]{0:T(1024)(128)(4,1)S(1)}, s32[]{:S(2)}) async-start(s8[8388608]{0:T(1024)(128)(4,1)} %bitcast.160), calls=%async_computation.5 | async-start | bytes 8388608
  225.7 18.1 %copy-start.8 = (f32[32,2048]{1,0:T(8,128)S(1)}, f32[32,2048]{1,0:T(8,128)}, u32[]{:S(2)}) copy-start(f32[32,2048]{1,0:T(8,128)} %param.16) | copy-start | bytes 786436
  228.6 6.6 %collective-permute-start.28 = (bf16[32,2048]{1,0:T(8,128)(2,1)S(1)}, bf16[32,2048]{1,0:T(8,128)(2,1)S(1)}, u32[]{:S(2)}, u32[]{:S(2)}) collective-permute-start(bf16[32,2048]{1,0:T(8,128)(2,1)S(1)} %constant_dynamic-update-slice_fusion.17), channel_id=1, source_target_pairs={{0,4},{1,5},{2,6},{3,7},{4,0},{5,1},{6,2},{7,3},{8,12},{9,13},{10,... | collective-permute-start | bytes 393224 | tf_op jit(solution)/shard_map/ppermute | solution.py:81
  235.2 6.3 %collective-permute-start.31 = (bf16[32,2048]{1,0:T(8,128)(2,1)S(1)}, bf16[32,2048]{1,0:T(8,128)(2,1)S(1)}, u32[]{:S(2)}, u32[]{:S(2)}) collective-permute-start(bf16[32,2048]{1,0:T(8,128)(2,1)S(1)} %add_convert_fusion.5), channel_id=1, source_target_pairs={{0,3},{1,2},{2,1},{3,0},{4,7},{5,6},{6,5},{7,4},{8,11},{9,10},{10,... | collective-permute-start | bytes 393224 | tf_op jit(solution)/shard_map/ppermute | solution.py:81
  236.6 6.5 %collective-permute-start.30 = (bf16[32,2048]{1,0:T(8,128)(2,1)S(1)}, bf16[32,2048]{1,0:T(8,128)(2,1)S(1)}, u32[]{:S(2)}, u32[]{:S(2)}) collective-permute-start(bf16[32,2048]{1,0:T(8,128)(2,1)S(1)} %add_convert_fusion.5), channel_id=1, source_target_pairs={{0,2},{1,3},{2,0},{3,1},{4,6},{5,7},{6,4},{7,5},{8,10},{9,11},{10,... | collective-permute-start | bytes 393224 | tf_op jit(solution)/shard_map/ppermute | solution.py:81
  237.5 6.3 %collective-permute-start.29 = (bf16[32,2048]{1,0:T(8,128)(2,1)S(1)}, bf16[32,2048]{1,0:T(8,128)(2,1)S(1)}, u32[]{:S(2)}, u32[]{:S(2)}) collective-permute-start(bf16[32,2048]{1,0:T(8,128)(2,1)S(1)} %add_convert_fusion.5), channel_id=1, source_target_pairs={{0,1},{1,0},{2,3},{3,2},{4,5},{5,4},{6,7},{7,6},{8,9},{9,8},{10,11... | collective-permute-start | bytes 393224 | tf_op jit(solution)/shard_map/ppermute | solution.py:81
  250.7 6.6 %collective-permute-start.32 = (bf16[32,2048]{1,0:T(8,128)(2,1)S(1)}, bf16[32,2048]{1,0:T(8,128)(2,1)S(1)}, u32[]{:S(2)}, u32[]{:S(2)}) collective-permute-start(bf16[32,2048]{1,0:T(8,128)(2,1)S(1)} %convolution_convert_fusion.2), channel_id=1, source_target_pairs={{0,4},{1,5},{2,6},{3,7},{4,0},{5,1},{6,2},{7,3},{8,12},{9,13},{10,... | collective-permute-start | bytes 393224 | tf_op jit(solution)/shard_map/ppermute | solution.py:81
  257.3 6.3 %collective-permute-start.35 = (bf16[32,2048]{1,0:T(8,128)(2,1)S(1)}, bf16[32,2048]{1,0:T(8,128)(2,1)S(1)}, u32[]{:S(2)}, u32[]{:S(2)}) collective-permute-start(bf16[32,2048]{1,0:T(8,128)(2,1)S(1)} %add_convert_fusion.3), channel_id=1, source_target_pairs={{0,3},{1,2},{2,1},{3,0},{4,7},{5,6},{6,5},{7,4},{8,11},{9,10},{10,... | collective-permute-start | bytes 393224 | tf_op jit(solution)/shard_map/ppermute | solution.py:81
  258.7 6.5 %collective-permute-start.34 = (bf16[32,2048]{1,0:T(8,128)(2,1)S(1)}, bf16[32,2048]{1,0:T(8,128)(2,1)S(1)}, u32[]{:S(2)}, u32[]{:S(2)}) collective-permute-start(bf16[32,2048]{1,0:T(8,128)(2,1)S(1)} %add_convert_fusion.3), channel_id=1, source_target_pairs={{0,2},{1,3},{2,0},{3,1},{4,6},{5,7},{6,4},{7,5},{8,10},{9,11},{10,... | collective-permute-start | bytes 393224 | tf_op jit(solution)/shard_map/ppermute | solution.py:81
  260.1 5.8 %collective-permute-start.33 = (bf16[32,2048]{1,0:T(8,128)(2,1)S(1)}, bf16[32,2048]{1,0:T(8,128)(2,1)S(1)}, u32[]{:S(2)}, u32[]{:S(2)}) collective-permute-start(bf16[32,2048]{1,0:T(8,128)(2,1)S(1)} %add_convert_fusion.3), channel_id=1, source_target_pairs={{0,1},{1,0},{2,3},{3,2},{4,5},{5,4},{6,7},{7,6},{8,9},{9,8},{10,11... | collective-permute-start | bytes 393224 | tf_op jit(solution)/shard_map/ppermute | solution.py:81
  (20 other events, 115.5 us)
where the time goes:
time: 268 us; the launch traced here: 267 us
  waiting for transfers between devices  95.3 us (36%)
  starting transfers between devices  72.8 us (27%)
  matrix products  45.7 us (17%)
  other arithmetic  20.8 us (8%)
  local copies, waits for them, and re-layouts  18.3 us (7%)
  blocking collectives  12.6 us (5%)
    ppermute x25, waiting for transfers between devices, send(): return lax.ppermute(x, AXES, pairs)  66.6 us
    ppermute x25, starting transfers between devices, send(): return lax.ppermute(x, AXES, pairs)  31.4 us
    dot_general x14, matrix products, matmul(): return jnp.dot(a, b, preferred_element_type=F32)  27.3 us
    ppermute x8, waiting for transfers between devices, from_xor(): return lax.ppermute(v, 'tensor', [(s, s ^ j) for s in range(8)]).astype(F32)  21 us
    ppermute x3, starting transfers between devices, doubling_blocks(): lax.ppermute(got, 'tensor', [(s, s ^ 1 << bit) for s in range(8)])  16.4 us
    all_to_all x1, blocking collectives, shards(): q_all = lax.all_to_all(q_heads, 'dp', 0, 0, tiled=True)  12.6 us
    dot_general x4, matrix products, shards(): lax.dot_general(wide[i], values[i], (((2,), (1,)), ((0,), (0,))), preferr...  10.4 us
    ppermute x8, starting transfers between devices, from_xor(): return lax.ppermute(v, 'tensor', [(s, s ^ j) for s in range(8)]).astype(F32)  9.15 us
  transfers between devices with their start and end apart: 39, of which 20 were waited for; matrix products, arithmetic and copies ran while one was open for 23% of the time, Pallas kernels for 0%

commit v1 on v0

--- a/solution.py
+++ b/solution.py
@@ -1,6 +1,8 @@
 import jax
 import jax.numpy as jnp
 from jax import lax
+from jax.experimental import pallas as pl
+from jax.experimental.pallas import tpu as pltpu
 from jax.sharding import PartitionSpec as P
 
 HEAD_DIM = 128
@@ -91,6 +93,45 @@
     beside_below, beside_above = send(beside, Y_UP), send(beside, Y_DOWN)
     beside_far = send(far, X_LO)
     return [x, above, far, below], [beside, beside_above, beside_far, beside_below]
+
+
+def back_kernel(inner, weights, out, held, arrived):
+    pieces = held.shape[0]
+    rows = held.shape[1]
+    copies = [
+        pltpu.make_async_copy(weights.at[pl.ds(k * rows, rows)], held.at[k], arrived.at[k])
+        for k in range(pieces)
+    ]
+    for copy in copies:
+        copy.start()
+    total = None
+    for k in range(pieces):
+        copies[k].wait()
+        part = matmul(inner[:, k * rows : (k + 1) * rows], held[k])
+        total = part if total is None else total + part
+    out[...] = total.astype(out.dtype)
+
+
+def back_project(inner, weights):
+    pieces = 4
+    depth, width = weights.shape
+    vmem = pl.BlockSpec(memory_space=pltpu.VMEM)
+    return pl.pallas_call(
+        back_kernel,
+        out_shape=jax.ShapeDtypeStruct((inner.shape[0], width), BF16),
+        in_specs=[vmem, pl.BlockSpec(memory_space=pl.ANY)],
+        out_specs=vmem,
+        scratch_shapes=[
+            pltpu.VMEM((pieces, depth // pieces, width), BF16),
+            pltpu.SemaphoreType.DMA((pieces,)),
+        ],
+        compiler_params=pltpu.CompilerParams(vmem_limit_bytes=24 * 2**20),
+        cost_estimate=pl.CostEstimate(
+            flops=2 * inner.shape[0] * depth * width,
+            bytes_accessed=2 * depth * width,
+            transcendentals=0,
+        ),
+    )(inner, weights)
 
 
 def shards(
@@ -181,7 +222,7 @@
     mid = queries + matmul(attended, w_out)
     mnorm = layer_norm(mid).astype(BF16)
     inner = jax.nn.gelu(matmul(mnorm, w_in)).astype(BF16)
-    back = tensor_sum(matmul(inner, w_back).astype(BF16))
+    back = tensor_sum(back_project(inner, w_back))
     return (mid + back).astype(BF16)
 
 

time: 268 us -> 265 us (0.989)
  matrix products: 45.7 us -> 40.3 us
  local copies, waits for them, and re-layouts: 18.3 us -> 21.1 us
    dot_general x14, matrix products: 27.3 us -> 22 us  [matmul(): return jnp.dot(a, b, preferred_element_type=F32)]
    unnamed x94 -> x100, local copies, waits for them, and re-layouts: 8.15 us -> 11 us
  transfers between devices with their start and end apart: 39 -> 39, of which waited for: 20 -> 21; matrix products, arithmetic and copies ran while one was open for 23% -> 22% of each run, Pallas kernels for 0% -> 0%
where the time goes in v1:
time: 265 us; the launch traced here: 264 us
  waiting for transfers between devices  95.1 us (36%)
  starting transfers between devices  72.5 us (27%)
  matrix products  40.3 us (15%)
  local copies, waits for them, and re-layouts  21.1 us (8%)
  other arithmetic  19.8 us (7%)
  blocking collectives  12.6 us (5%)
    ppermute x25, waiting for transfers between devices, send(): return lax.ppermute(x, AXES, pairs)  66.3 us
    ppermute x25, starting transfers between devices, send(): return lax.ppermute(x, AXES, pairs)  31.4 us
    dot_general x14, matrix products, matmul(): return jnp.dot(a, b, preferred_element_type=F32)  22 us
    ppermute x8, waiting for transfers between devices, from_xor(): return lax.ppermute(v, 'tensor', [(s, s ^ j) for s in range(8)]).astype(F32)  21.2 us
    ppermute x3, starting transfers between devices, doubling_blocks(): lax.ppermute(got, 'tensor', [(s, s ^ 1 << bit) for s in range(8)])  16.4 us
    all_to_all x1, blocking collectives, shards(): q_all = lax.all_to_all(q_heads, 'dp', 0, 0, tiled=True)  12.6 us
    unnamed x100, local copies, waits for them, and re-layouts  11 us
    dot_general x4, matrix products, shards(): lax.dot_general(wide[i], values[i], (((2,), (1,)), ((0,), (0,))), preferr...  10.4 us
  transfers between devices with their start and end apart: 39, of which 21 were waited for; matrix products, arithmetic and copies ran while one was open for 22% of the time, Pallas kernels for 0%

profile of v1, /device:TPU:0, one launch (start us, length us, event | category | flops | bytes accessed | tf_op | source)
XLA Modules:
  0.0 263.7 jit_solution(8486365356997359347)
XLA Ops:
  5.9 4.2 %collective-permute-start.1 = (bf16[384,512]{1,0:T(8,128)(2,1)}, bf16[384,512]{1,0:T(8,128)(2,1)}, u32[]{:S(2)}, u32[]{:S(2)}) collective-permute-start(bf16[384,512]{1,0:T(8,128)(2,1)} %pad_maximum_fusion.5), channel_id=1, source_target_pairs={{0,4},{1,5},{2,6},{3,7},{4,68},{5,69},{6,70},{7,71},{8,12},{9,13},... | collective-permute-start | bytes 1179656 | tf_op jit(solution)/shard_map/ppermute | solution.py:52
  10.5 2.0 collective-permute-start.5
  12.5 3.0 %collective-permute-start.10 = (bf16[1536,384]{1,0:T(8,128)(2,1)}, bf16[1536,384]{1,0:T(8,128)(2,1)}, u32[]{:S(2)}, u32[]{:S(2)}) collective-permute-start(bf16[1536,384]{1,0:T(8,128)(2,1)} %param.13), channel_id=1, source_target_pairs={{0,48},{1,49},{2,50},{3,51},{4,52},{5,53},{6,54},{7,55},{8,56},{9,... | collective-permute-start | bytes 3538952 | tf_op jit(solution)/shard_map/ppermute | solution.py:52
  16.4 2.9 %collective-permute-done.1 = bf16[384,512]{1,0:T(8,128)(2,1)} collective-permute-done((bf16[384,512]{1,0:T(8,128)(2,1)}, bf16[384,512]{1,0:T(8,128)(2,1)}, u32[]{:S(2)}, u32[]{:S(2)}) %collective-permute-start.1) | collective-permute-done | bytes 393248 | tf_op jit(solution)/shard_map/ppermute | solution.py:52
  19.3 3.9 %collective-permute-start.6 = (bf16[2,32,256]{2,1,0:T(8,128)(2,1)S(1)}, bf16[2,32,256]{2,1,0:T(8,128)(2,1)S(1)}, u32[]{:S(2)}, u32[]{:S(2)}) collective-permute-start(bf16[2,32,256]{2,1,0:T(8,128)(2,1)S(1)} %pad_maximum_fusion.9), channel_id=1, source_target_pairs={{0,2},{1,3},{2,0},{3,1},{4,6},{5,7},{6,4},{7,5},{8,10},{9,11},{10,... | collective-permute-start | bytes 98312 | tf_op jit(solution)/shard_map/ppermute | solution.py:35
  26.9 10.6 %collective-permute-start.7 = (bf16[4,32,256]{2,1,0:T(8,128)(2,1)S(1)}, bf16[4,32,256]{2,1,0:T(8,128)(2,1)S(1)}, u32[]{:S(2)}, u32[]{:S(2)}) collective-permute-start(bf16[4,32,256]{2,1,0:T(8,128)(2,1)S(1)} %pad_maximum_fusion.8), channel_id=1, source_target_pairs={{0,4},{1,5},{2,6},{3,7},{4,0},{5,1},{6,2},{7,3},{8,12},{9,13},{10,... | collective-permute-start | bytes 196616 | tf_op jit(solution)/shard_map/ppermute | solution.py:35
  37.5 2.2 collective-permute-done.7
  39.9 12.6 %all_to_all.42 = bf16[16,32,128]{2,1,0:T(8,128)(2,1)} all-to-all(bf16[16,32,128]{2,1,0:T(8,128)(2,1)S(1)} %bitcast.175), channel_id=1, replica_groups=mesh['dp'=16,'tensor'=8] {'dp'}, dimensions={0} | all-to-all | bytes 262144 | tf_op jit(solution)/shard_map/all_to_all | solution.py:163
  56.0 2.2 collective-permute-start.9
  61.6 5.8 %collective-permute-done.8 = bf16[192,1024]{1,0:T(8,128)(2,1)} collective-permute-done((bf16[192,1024]{1,0:T(8,128)(2,1)}, bf16[192,1024]{1,0:T(8,128)(2,1)}, u32[]{:S(2)}, u32[]{:S(2)}) %collective-permute-start.8) | collective-permute-done | bytes 393248 | tf_op jit(solution)/shard_map/ppermute | solution.py:52
  70.4 6.0 %collective-permute-done.12 = bf16[768,384]{1,0:T(8,128)(2,1)S(1)} collective-permute-done((bf16[768,384]{1,0:T(8,128)(2,1)S(1)}, bf16[768,384]{1,0:T(8,128)(2,1)S(1)}, u32[]{:S(2)}, u32[]{:S(2)}) %collective-permute-start.12) | collective-permute-done | bytes 589856 | tf_op jit(solution)/shard_map/ppermute | solution.py:52
  76.5 2.3 fusion.69
  80.0 2.8 %fusion.2 = f32[1536,512]{0,1:T(8,128)S(1)} fusion(f32[512,1536]{1,0:T(8,128)S(1)} %fusion.69, bf16[1536,384]{1,0:T(8,128)(2,1)} %collective-permute-done.10, bf16[4,384,512]{2,1,0:T(8,128)(2,1)S(1)} %get-tuple-element.21, s32[]{:T(128)S(6)} %select_n.263), kind=kOutput, calls=%fused_computation.10 | convolution fusion | flops 604766208 | bytes 7864324 | tf_op jit(solution)/shard_map/dot_general | solution.py:22
  83.9 1.6 copy-done.3
  86.5 1.8 copy.23
  89.1 1.8 slice_add_fusion.1
  92.3 2.3 fusion.64
  95.7 2.4 fusion.3
  102.5 2.2 convolution_convert_fusion
  104.7 4.4 %all-to-all-start.1 = ((bf16[16,32,2304]{2,1,0:T(8,128)(2,1)}), bf16[16,32,2304]{2,1,0:T(8,128)(2,1)}, u32[]{:S(2)}, u32[]{:S(2)}) async-start(bf16[16,32,2304]{2,1,0:T(8,128)(2,1)} %bitcast.161), calls=%async_computation.1 | async-start | bytes 4718592 | tf_op jit(solution)/shard_map/all_to_all | solution.py:190
  109.2 1.8 slice_add_fusion
  112.3 1.9 collective-permute-start.16
  114.3 33.6 %collective-permute-done.16 = bf16[1536,128]{0,1:T(8,128)(2,1)} collective-permute-done((bf16[1536,128]{0,1:T(8,128)(2,1)S(1)}, bf16[1536,128]{0,1:T(8,128)(2,1)}, u32[]{:S(2)}, u32[]{:S(2)}) %collective-permute-start.16) | collective-permute-done | bytes 393248 | tf_op jit(solution)/shard_map/ppermute | solution.py:52
  150.0 4.6 %collective-permute-start.19 = (bf16[2304,128]{0,1:T(8,128)(2,1)}, bf16[2304,128]{0,1:T(8,128)(2,1)S(1)}, u32[]{:S(2)}, u32[]{:S(2)}) collective-permute-start(bf16[2304,128]{0,1:T(8,128)(2,1)} %pad_maximum_fusion.4), channel_id=1, source_target_pairs={{0,16},{1,17},{2,18},{3,19},{4,20},{5,21},{6,22},{7,23},{8,24},{9,... | collective-permute-start | bytes 1769480 | tf_op jit(solution)/shard_map/ppermute | solution.py:52
  155.1 2.8 %fusion.7 = f32[512,768]{1,0:T(8,128)S(1)} fusion(bf16[768,1536]{1,0:T(8,128)(2,1)S(1)} %copy-done, bf16[512,2304]{1,0:T(8,128)(2,1)} %bitcast.20), kind=kOutput, calls=%fused_computation.36 | convolution fusion | flops 1207959552 | bytes 5505024 | tf_op jit(solution)/shard_map/dot_general | solution.py:26
  158.0 9.4 %collective-permute-done.19 = bf16[2304,128]{0,1:T(8,128)(2,1)S(1)} collective-permute-done((bf16[2304,128]{0,1:T(8,128)(2,1)}, bf16[2304,128]{0,1:T(8,128)(2,1)S(1)}, u32[]{:S(2)}, u32[]{:S(2)}) %collective-permute-start.19) | collective-permute-done | bytes 589856 | tf_op jit(solution)/shard_map/ppermute | solution.py:52
  168.1 2.4 collective-permute-start.20
  170.5 2.9 %add_convert_fusion = bf16[512,768]{1,0:T(8,128)(2,1)} fusion(f32[512,768]{1,0:T(8,128)S(1)} %fusion.7, bf16[768,768]{1,0:T(8,128)(2,1)S(1)} %copy-done.28, bf16[512,2304]{1,0:T(8,128)(2,1)} %bitcast.20), kind=kOutput, calls=%fused_computation.35 | convolution fusion | flops 604766208 | bytes 4325376 | tf_op jit(solution)/shard_map/dot_general | solution.py:26
  173.4 3.9 %all-to-all-start.2 = ((bf16[8,64,768]{2,1,0:T(8,128)(2,1)}), bf16[8,64,768]{2,1,0:T(8,128)(2,1)S(1)}, u32[]{:S(2)}, u32[]{:S(2)}) async-start(bf16[8,64,768]{2,1,0:T(8,128)(2,1)} %bitcast.173), calls=%async_computation.2 | async-start | bytes 1572864 | tf_op jit(solution)/shard_map/all_to_all | solution.py:196
  180.5 2.1 collective-permute-start.23
  183.3 5.1 %collective-permute-done.21 = bf16[1152,128]{0,1:T(8,128)(2,1)S(1)} collective-permute-done((bf16[1152,128]{0,1:T(8,128)(2,1)S(1)}, bf16[1152,128]{0,1:T(8,128)(2,1)S(1)}, u32[]{:S(2)}, u32[]{:S(2)}) %collective-permute-start.21) | collective-permute-done | bytes 294944 | tf_op jit(solution)/shard_map/ppermute | solution.py:52
  191.2 7.3 %all-to-all-start.3 = ((bf16[8,64,768]{2,1,0:T(8,128)(2,1)}), bf16[8,64,768]{2,1,0:T(8,128)(2,1)}, u32[]{:S(2)}, u32[]{:S(2)}) async-start(bf16[8,64,768]{2,1,0:T(8,128)(2,1)} %broadcast_in_dim.5), calls=%async_computation.3 | async-start | bytes 1572864 | tf_op jit(solution)/shard_map/all_to_all | solution.py:200
  198.5 3.1 %pad_maximum_fusion.1 = bf16[4,2304,128]{1,2,0:T(8,128)(2,1)} fusion(bf16[1,2304,128]{1,2,0:T(8,128)(2,1)S(1)} %bitcast.168, bf16[1,2304,128]{1,2,0:T(8,128)(2,1)} %bitcast.28, bf16[1,2304,128]{1,2,0:T(8,128)(2,1)} %bitcast.27, bf16[1,2304,128]{1,2,0:T(8,128)(2,1)} %bitcast.26), kind=kLoop, calls=%fused_computation.24 | loop fusion | flops 3538944 | bytes 4718592 | tf_op jit(solution)/shard_map/stack | solution.py:193
  203.0 3.3 %pad_maximum_fusion.2 = bf16[4,2304,128]{1,2,0:T(8,128)(2,1)} fusion(bf16[1,2304,128]{1,2,0:T(8,128)(2,1)} %bitcast.34, bf16[1,2304,128]{1,2,0:T(8,128)(2,1)} %bitcast.33, bf16[1,2304,128]{1,2,0:T(8,128)(2,1)} %bitcast.32, bf16[1,2304,128]{1,2,0:T(8,128)(2,1)} %bitcast.31), kind=kLoop, calls=%fused_computation.25 | loop fusion | flops 3538944 | bytes 4718592 | tf_op jit(solution)/shard_map/stack | solution.py:193
  206.2 5.0 %all-to-all-done.3 = bf16[8,64,768]{2,1,0:T(8,128)(2,1)} async-done(((bf16[8,64,768]{2,1,0:T(8,128)(2,1)}), bf16[8,64,768]{2,1,0:T(8,128)(2,1)}, u32[]{:S(2)}, u32[]{:S(2)}) %all-to-all-start.3) | async-done | bytes 786464 | tf_op jit(solution)/shard_map/all_to_all | solution.py:200
  211.3 2.9 %convolution_convert_fusion.3 = bf16[512,768]{1,0:T(8,128)(2,1)S(1)} fusion(bf16[512,768]{1,0:T(8,128)(2,1)} %bitcast.24, s32[512]{0:T(512)S(1)} %get-tuple-element.40, s32[512]{0:T(512)S(1)} %get-tuple-element.41, s32[]{:T(128)S(6)} %select_n.242, s32[]{:T(128)S(6)} %select_n.240, s32[512]{0:T(512)S(1)} %get-tuple-element.39, ...), kind=kOutput, calls=%fused_computation.50 | convolution fusion | flops 418512896 | bytes 1582092 | tf_op jit(solution)/shard_map/dot_general | solution.py:22
  216.5 2.7 %convolution_convert_fusion.7 = bf16[4,32,128]{2,1,0:T(8,128)(2,1)S(1)} fusion(bf16[4,32,2304]{2,1,0:T(8,128)(2,1)S(1)} %bitcast.165, bf16[4,2304,128]{1,2,0:T(8,128)(2,1)} %pad_maximum_fusion.1), kind=kOutput, calls=%fused_computation.54 | convolution fusion | flops 75513856 | bytes 2981888 | tf_op jit(solution)/shard_map/dot_general | solution.py:211
  219.2 2.7 %convolution_convert_fusion.6 = bf16[4,32,128]{2,1,0:T(8,128)(2,1)S(1)} fusion(bf16[4,32,2304]{2,1,0:T(8,128)(2,1)S(1)} %bitcast.164, bf16[4,2304,128]{1,2,0:T(8,128)(2,1)} %pad_maximum_fusion.2), kind=kOutput, calls=%fused_computation.53 | convolution fusion | flops 75513856 | bytes 2981888 | tf_op jit(solution)/shard_map/dot_general | solution.py:211
  221.9 2.5 convolution_convert_fusion.5
  224.5 2.6 convolution_convert_fusion.4
  227.6 6.3 %collective-permute-done.28 = bf16[32,2048]{1,0:T(8,128)(2,1)S(1)} collective-permute-done((bf16[32,2048]{1,0:T(8,128)(2,1)S(1)}, bf16[32,2048]{1,0:T(8,128)(2,1)S(1)}, u32[]{:S(2)}, u32[]{:S(2)}) %collective-permute-start.28) | collective-permute-done | bytes 131104 | tf_op jit(solution)/shard_map/ppermute | solution.py:83
  236.2 1.9 collective-permute-start.29
  238.1 2.1 collective-permute-done.31
  240.2 1.6 collective-permute-done.30
  242.5 1.6 fusion.136
  248.2 6.2 %collective-permute-done.32 = bf16[32,2048]{1,0:T(8,128)(2,1)S(1)} collective-permute-done((bf16[32,2048]{1,0:T(8,128)(2,1)S(1)}, bf16[32,2048]{1,0:T(8,128)(2,1)S(1)}, u32[]{:S(2)}, u32[]{:S(2)}) %collective-permute-start.32) | collective-permute-done | bytes 131104 | tf_op jit(solution)/shard_map/ppermute | solution.py:83
  258.6 2.1 collective-permute-done.35
  260.7 1.6 collective-permute-done.34
  (210 shorter events, 59.6 us)
Async XLA Ops:
  0.0 155.1 %copy-start = (bf16[768,1536]{1,0:T(8,128)(2,1)S(1)}, bf16[768,1536]{1,0:T(8,128)(2,1)}, u32[]{:S(2)}) copy-start(bf16[768,1536]{1,0:T(8,128)(2,1)} %param.11) | copy-start | bytes 7077892
  2.1 1.5 collective-permute-start
  3.4 12.1 %copy-start.21 = (bf16[384,128]{1,0:T(8,128)(2,1)}, bf16[384,128]{1,0:T(8,128)(2,1)S(1)}, u32[]{:S(2)}) copy-start(bf16[384,128]{1,0:T(8,128)(2,1)S(1)} %get-tuple-element.30) | copy-start | bytes 294916
  3.7 11.8 %copy-start.22 = (bf16[384,128]{1,0:T(8,128)(2,1)}, bf16[384,128]{1,0:T(8,128)(2,1)S(1)}, u32[]{:S(2)}) copy-start(bf16[384,128]{1,0:T(8,128)(2,1)S(1)} %get-tuple-element.31) | copy-start | bytes 294916
  4.5 11.9 %collective-permute-start.2 = (bf16[384,512]{1,0:T(8,128)(2,1)}, bf16[384,512]{1,0:T(8,128)(2,1)}, u32[]{:S(2)}, u32[]{:S(2)}) collective-permute-start(bf16[384,512]{1,0:T(8,128)(2,1)} %pad_maximum_fusion.5), channel_id=1, source_target_pairs={{4,64},{5,65},{6,66},{7,67},{12,72},{13,73},{14,74},{15,75},{20,80... | collective-permute-start | bytes 1179656 | tf_op jit(solution)/shard_map/ppermute | solution.py:52
  5.9 13.4 %collective-permute-start.1 = (bf16[384,512]{1,0:T(8,128)(2,1)}, bf16[384,512]{1,0:T(8,128)(2,1)}, u32[]{:S(2)}, u32[]{:S(2)}) collective-permute-start(bf16[384,512]{1,0:T(8,128)(2,1)} %pad_maximum_fusion.5), channel_id=1, source_target_pairs={{0,4},{1,5},{2,6},{3,7},{4,68},{5,69},{6,70},{7,71},{8,12},{9,13},... | collective-permute-start | bytes 1179656 | tf_op jit(solution)/shard_map/ppermute | solution.py:52
  10.5 5.2 %collective-permute-start.5 = (bf16[1,32,256]{2,1,0:T(8,128)(2,1)S(1)}, bf16[1,32,256]{2,1,0:T(8,128)(2,1)}, u32[]{:S(2)}, u32[]{:S(2)}) collective-permute-start(bf16[1,32,256]{2,1,0:T(8,128)(2,1)S(1)} %fusion.10), channel_id=1, source_target_pairs={{0,1},{1,0},{2,3},{3,2},{4,5},{5,4},{6,7},{7,6},{8,9},{9,8},{10,11... | collective-permute-start | bytes 49160 | tf_op jit(solution)/shard_map/ppermute | solution.py:35
  12.5 45.8 %collective-permute-start.10 = (bf16[1536,384]{1,0:T(8,128)(2,1)}, bf16[1536,384]{1,0:T(8,128)(2,1)}, u32[]{:S(2)}, u32[]{:S(2)}) collective-permute-start(bf16[1536,384]{1,0:T(8,128)(2,1)} %param.13), channel_id=1, source_target_pairs={{0,48},{1,49},{2,50},{3,51},{4,52},{5,53},{6,54},{7,55},{8,56},{9,... | collective-permute-start | bytes 3538952 | tf_op jit(solution)/shard_map/ppermute | solution.py:52
  15.5 45.0 %collective-permute-start.11 = (bf16[1536,384]{1,0:T(8,128)(2,1)}, bf16[1536,384]{1,0:T(8,128)(2,1)S(1)}, u32[]{:S(2)}, u32[]{:S(2)}) collective-permute-start(bf16[1536,384]{1,0:T(8,128)(2,1)} %param.13), channel_id=1, source_target_pairs={{0,16},{1,17},{2,18},{3,19},{4,20},{5,21},{6,22},{7,23},{8,24},{9,... | collective-permute-start | bytes 3538952 | tf_op jit(solution)/shard_map/ppermute | solution.py:52
  19.3 7.6 %collective-permute-start.6 = (bf16[2,32,256]{2,1,0:T(8,128)(2,1)S(1)}, bf16[2,32,256]{2,1,0:T(8,128)(2,1)S(1)}, u32[]{:S(2)}, u32[]{:S(2)}) collective-permute-start(bf16[2,32,256]{2,1,0:T(8,128)(2,1)S(1)} %pad_maximum_fusion.9), channel_id=1, source_target_pairs={{0,2},{1,3},{2,0},{3,1},{4,6},{5,7},{6,4},{7,5},{8,10},{9,11},{10,... | collective-permute-start | bytes 98312 | tf_op jit(solution)/shard_map/ppermute | solution.py:35
  24.8 27.8 %copy-start.18 = (bf16[384,1024]{1,0:T(8,128)(2,1)}, bf16[384,1024]{1,0:T(8,128)(2,1)S(1)}, u32[]{:S(2)}) copy-start(bf16[384,1024]{1,0:T(8,128)(2,1)S(1)} %slice_dynamic-update-slice_fusion) | copy-start | bytes 2359300
  24.8 27.7 %collective-permute-start.4 = (bf16[384,1024]{1,0:T(8,128)(2,1)S(1)}, bf16[384,1024]{1,0:T(8,128)(2,1)S(1)}, u32[]{:S(2)}, u32[]{:S(2)}) collective-permute-start(bf16[384,1024]{1,0:T(8,128)(2,1)S(1)} %slice_dynamic-update-slice_fusion), channel_id=1, source_target_pairs={{0,3},{1,0},{2,1},{3,2},{4,7},{5,4},{6,5},{7,6},{8,11},{9,8},{10,9... | collective-permute-start | bytes 2359304 | tf_op jit(solution)/shard_map/ppermute | solution.py:52
  25.6 26.9 %collective-permute-start.3 = (bf16[384,1024]{1,0:T(8,128)(2,1)S(1)}, bf16[384,1024]{1,0:T(8,128)(2,1)S(1)}, u32[]{:S(2)}, u32[]{:S(2)}) collective-permute-start(bf16[384,1024]{1,0:T(8,128)(2,1)S(1)} %slice_dynamic-update-slice_fusion), channel_id=1, source_target_pairs={{0,1},{1,2},{2,3},{3,0},{4,5},{5,6},{6,7},{7,4},{8,9},{9,10},{10,1... | collective-permute-start | bytes 2359304 | tf_op jit(solution)/shard_map/ppermute | solution.py:52
  26.9 12.8 %collective-permute-start.7 = (bf16[4,32,256]{2,1,0:T(8,128)(2,1)S(1)}, bf16[4,32,256]{2,1,0:T(8,128)(2,1)S(1)}, u32[]{:S(2)}, u32[]{:S(2)}) collective-permute-start(bf16[4,32,256]{2,1,0:T(8,128)(2,1)S(1)} %pad_maximum_fusion.8), channel_id=1, source_target_pairs={{0,4},{1,5},{2,6},{3,7},{4,0},{5,1},{6,2},{7,3},{8,12},{9,13},{10,... | collective-permute-start | bytes 196616 | tf_op jit(solution)/shard_map/ppermute | solution.py:35
  55.0 12.4 %collective-permute-start.8 = (bf16[192,1024]{1,0:T(8,128)(2,1)}, bf16[192,1024]{1,0:T(8,128)(2,1)}, u32[]{:S(2)}, u32[]{:S(2)}) collective-permute-start(bf16[192,1024]{1,0:T(8,128)(2,1)} %slice.141), channel_id=1, source_target_pairs={{0,1},{1,2},{2,3},{3,0},{4,5},{5,6},{6,7},{7,4},{8,9},{9,10},{10,1... | collective-permute-start | bytes 1179656 | tf_op jit(solution)/shard_map/ppermute | solution.py:52
  56.0 11.4 %collective-permute-start.9 = (bf16[192,1024]{1,0:T(8,128)(2,1)}, bf16[192,1024]{1,0:T(8,128)(2,1)}, u32[]{:S(2)}, u32[]{:S(2)}) collective-permute-start(bf16[192,1024]{1,0:T(8,128)(2,1)} %slice.142), channel_id=1, source_target_pairs={{0,3},{1,0},{2,1},{3,2},{4,7},{5,4},{6,5},{7,6},{8,11},{9,8},{10,9... | collective-permute-start | bytes 1179656 | tf_op jit(solution)/shard_map/ppermute | solution.py:52
  59.4 20.5 %collective-permute-start.13 = (bf16[768,384]{1,0:T(8,128)(2,1)S(1)}, bf16[768,384]{1,0:T(8,128)(2,1)S(1)}, u32[]{:S(2)}, u32[]{:S(2)}) collective-permute-start(bf16[768,384]{1,0:T(8,128)(2,1)S(1)} %slice.178), channel_id=1, source_target_pairs={{0,48},{1,49},{2,50},{3,51},{4,52},{5,53},{6,54},{7,55},{8,56},{9,... | collective-permute-start | bytes 1769480 | tf_op jit(solution)/shard_map/ppermute | solution.py:52
  60.6 15.8 %collective-permute-start.12 = (bf16[768,384]{1,0:T(8,128)(2,1)S(1)}, bf16[768,384]{1,0:T(8,128)(2,1)S(1)}, u32[]{:S(2)}, u32[]{:S(2)}) collective-permute-start(bf16[768,384]{1,0:T(8,128)(2,1)S(1)} %slice.177), channel_id=1, source_target_pairs={{0,16},{1,17},{2,18},{3,19},{4,20},{5,21},{6,22},{7,23},{8,24},{9,... | collective-permute-start | bytes 1769480 | tf_op jit(solution)/shard_map/ppermute | solution.py:52
  86.5 2.6 collective-permute-start.14
  91.0 11.4 %collective-permute-start.17 = (bf16[1536,128]{0,1:T(8,128)(2,1)S(1)}, bf16[1536,128]{0,1:T(8,128)(2,1)S(1)}, u32[]{:S(2)}, u32[]{:S(2)}) collective-permute-start(bf16[1536,128]{0,1:T(8,128)(2,1)S(1)} %slice.236), channel_id=1, source_target_pairs={{0,64},{1,65},{2,66},{3,67},{4,68},{5,69},{6,70},{7,71},{8,72},{9,... | collective-permute-start | bytes 1179656 | tf_op jit(solution)/shard_map/ppermute | solution.py:52
  100.9 8.2 %collective-permute-start.15 = (bf16[1536,256]{0,1:T(8,128)(2,1)S(1)}, bf16[1536,256]{0,1:T(8,128)(2,1)}, u32[]{:S(2)}, u32[]{:S(2)}) collective-permute-start(bf16[1536,256]{0,1:T(8,128)(2,1)S(1)} %slice.234), channel_id=1, source_target_pairs={{0,8},{1,9},{2,10},{3,11},{4,12},{5,13},{6,14},{7,15},{8,0},{9,1},... | collective-permute-start | bytes 2359304 | tf_op jit(solution)/shard_map/ppermute | solution.py:52
  104.7 45.3 %all-to-all-start.1 = ((bf16[16,32,2304]{2,1,0:T(8,128)(2,1)}), bf16[16,32,2304]{2,1,0:T(8,128)(2,1)}, u32[]{:S(2)}, u32[]{:S(2)}) async-start(bf16[16,32,2304]{2,1,0:T(8,128)(2,1)} %bitcast.161), calls=%async_computation.1 | async-start | bytes 4718592 | tf_op jit(solution)/shard_map/all_to_all | solution.py:190
  112.3 35.6 %collective-permute-start.16 = (bf16[1536,128]{0,1:T(8,128)(2,1)S(1)}, bf16[1536,128]{0,1:T(8,128)(2,1)}, u32[]{:S(2)}, u32[]{:S(2)}) collective-permute-start(bf16[1536,128]{0,1:T(8,128)(2,1)S(1)} %slice.237), channel_id=1, source_target_pairs={{0,64},{1,65},{2,66},{3,67},{4,68},{5,69},{6,70},{7,71},{8,72},{9,... | collective-permute-start | bytes 1179656 | tf_op jit(solution)/shard_map/ppermute | solution.py:52
  150.0 17.3 %collective-permute-start.19 = (bf16[2304,128]{0,1:T(8,128)(2,1)}, bf16[2304,128]{0,1:T(8,128)(2,1)S(1)}, u32[]{:S(2)}, u32[]{:S(2)}) collective-permute-start(bf16[2304,128]{0,1:T(8,128)(2,1)} %pad_maximum_fusion.4), channel_id=1, source_target_pairs={{0,16},{1,17},{2,18},{3,19},{4,20},{5,21},{6,22},{7,23},{8,24},{9,... | collective-permute-start | bytes 1769480 | tf_op jit(solution)/shard_map/ppermute | solution.py:52
  154.6 15.9 %copy-start.28 = (bf16[768,768]{1,0:T(8,128)(2,1)S(1)}, bf16[768,768]{1,0:T(8,128)(2,1)}, u32[]{:S(2)}) copy-start(bf16[768,768]{1,0:T(8,128)(2,1)} %param.12) | copy-start | bytes 3538948
  154.6 24.7 %collective-permute-start.22 = (bf16[2304,128]{0,1:T(8,128)(2,1)}, bf16[2304,128]{0,1:T(8,128)(2,1)}, u32[]{:S(2)}, u32[]{:S(2)}) collective-permute-start(bf16[2304,128]{0,1:T(8,128)(2,1)} %pad_maximum_fusion.4), channel_id=1, source_target_pairs={{0,64},{1,65},{2,66},{3,67},{4,68},{5,69},{6,70},{7,71},{8,72},{9,... | collective-permute-start | bytes 1769480 | tf_op jit(solution)/shard_map/ppermute | solution.py:52
  155.1 22.2 %collective-permute-start.18 = (bf16[2304,128]{0,1:T(8,128)(2,1)}, bf16[2304,128]{0,1:T(8,128)(2,1)}, u32[]{:S(2)}, u32[]{:S(2)}) collective-permute-start(bf16[2304,128]{0,1:T(8,128)(2,1)} %pad_maximum_fusion.4), channel_id=1, source_target_pairs={{0,48},{1,49},{2,50},{3,51},{4,52},{5,53},{6,54},{7,55},{8,56},{9,... | collective-permute-start | bytes 1769480 | tf_op jit(solution)/shard_map/ppermute | solution.py:52
  168.1 14.4 %collective-permute-start.20 = (bf16[1152,128]{0,1:T(8,128)(2,1)}, bf16[1152,128]{0,1:T(8,128)(2,1)S(1)}, u32[]{:S(2)}, u32[]{:S(2)}) collective-permute-start(bf16[1152,128]{0,1:T(8,128)(2,1)} %slice.188), channel_id=1, source_target_pairs={{0,16},{1,17},{2,18},{3,19},{4,20},{5,21},{6,22},{7,23},{8,24},{9,... | collective-permute-start | bytes 884744 | tf_op jit(solution)/shard_map/ppermute | solution.py:52
  173.4 16.3 %all-to-all-start.2 = ((bf16[8,64,768]{2,1,0:T(8,128)(2,1)}), bf16[8,64,768]{2,1,0:T(8,128)(2,1)S(1)}, u32[]{:S(2)}, u32[]{:S(2)}) async-start(bf16[8,64,768]{2,1,0:T(8,128)(2,1)} %bitcast.173), calls=%async_computation.2 | async-start | bytes 1572864 | tf_op jit(solution)/shard_map/all_to_all | solution.py:196
  177.3 12.5 %copy-start.24 = (f32[1,32,768]{2,1,0:T(8,128)S(1)}, f32[1,32,768]{2,1,0:T(8,128)}, u32[]{:S(2)}) copy-start(f32[1,32,768]{2,1,0:T(8,128)} %param.18) | copy-start | bytes 294916
  178.4 10.0 %collective-permute-start.21 = (bf16[1152,128]{0,1:T(8,128)(2,1)S(1)}, bf16[1152,128]{0,1:T(8,128)(2,1)S(1)}, u32[]{:S(2)}, u32[]{:S(2)}) collective-permute-start(bf16[1152,128]{0,1:T(8,128)(2,1)S(1)} %slice.189), channel_id=1, source_target_pairs={{0,48},{1,49},{2,50},{3,51},{4,52},{5,53},{6,54},{7,55},{8,56},{9,... | collective-permute-start | bytes 884744 | tf_op jit(solution)/shard_map/ppermute | solution.py:52
  179.3 22.4 %collective-permute-start.25 = (bf16[2304,128]{0,1:T(8,128)(2,1)}, bf16[2304,128]{0,1:T(8,128)(2,1)}, u32[]{:S(2)}, u32[]{:S(2)}) collective-permute-start(bf16[2304,128]{0,1:T(8,128)(2,1)} %collective-permute-done.22), channel_id=1, source_target_pairs={{0,16},{1,17},{2,18},{3,19},{4,20},{5,21},{6,22},{7,23},{8,24},{9,... | collective-permute-start | bytes 1769480 | tf_op jit(solution)/shard_map/ppermute | solution.py:52
  180.5 21.2 %collective-permute-start.23 = (bf16[2304,128]{0,1:T(8,128)(2,1)}, bf16[2304,128]{0,1:T(8,128)(2,1)}, u32[]{:S(2)}, u32[]{:S(2)}) collective-permute-start(bf16[2304,128]{0,1:T(8,128)(2,1)} %collective-permute-done.22), channel_id=1, source_target_pairs={{0,48},{1,49},{2,50},{3,51},{4,52},{5,53},{6,54},{7,55},{8,56},{9,... | collective-permute-start | bytes 1769480 | tf_op jit(solution)/shard_map/ppermute | solution.py:52
  189.1 13.8 %collective-permute-start.24 = (bf16[2304,128]{0,1:T(8,128)(2,1)}, bf16[2304,128]{0,1:T(8,128)(2,1)}, u32[]{:S(2)}, u32[]{:S(2)}) collective-permute-start(bf16[2304,128]{0,1:T(8,128)(2,1)} %constant_dynamic-update-slice_fusion.15), channel_id=1, source_target_pairs={{0,64},{1,65},{2,66},{3,67},{4,68},{5,69},{6,70},{7,71},{8,72},{9,... | collective-permute-start | bytes 1769480 | tf_op jit(solution)/shard_map/ppermute | solution.py:52
  191.2 20.1 %all-to-all-start.3 = ((bf16[8,64,768]{2,1,0:T(8,128)(2,1)}), bf16[8,64,768]{2,1,0:T(8,128)(2,1)}, u32[]{:S(2)}, u32[]{:S(2)}) async-start(bf16[8,64,768]{2,1,0:T(8,128)(2,1)} %broadcast_in_dim.5), calls=%async_computation.3 | async-start | bytes 1572864 | tf_op jit(solution)/shard_map/all_to_all | solution.py:200
  201.7 20.2 %collective-permute-start.26 = (bf16[4,2304,128]{1,2,0:T(8,128)(2,1)}, bf16[4,2304,128]{1,2,0:T(8,128)(2,1)}, u32[]{:S(2)}, u32[]{:S(2)}) collective-permute-start(bf16[4,2304,128]{1,2,0:T(8,128)(2,1)} %pad_maximum_fusion.1), channel_id=1, source_target_pairs={{0,8},{1,9},{2,10},{3,11},{4,12},{5,13},{6,14},{7,15},{8,0},{9,1},... | collective-permute-start | bytes 7077896 | tf_op jit(solution)/shard_map/ppermute | solution.py:52
  206.2 18.2 %collective-permute-start.27 = (bf16[4,2304,128]{1,2,0:T(8,128)(2,1)}, bf16[4,2304,128]{1,2,0:T(8,128)(2,1)}, u32[]{:S(2)}, u32[]{:S(2)}) collective-permute-start(bf16[4,2304,128]{1,2,0:T(8,128)(2,1)} %pad_maximum_fusion.2), channel_id=1, source_target_pairs={{0,8},{1,9},{2,10},{3,11},{4,12},{5,13},{6,14},{7,15},{8,0},{9,1},... | collective-permute-start | bytes 7077896 | tf_op jit(solution)/shard_map/ppermute | solution.py:52
  216.3 26.1 %slice-start = ((s8[8388608]{0:T(1024)(128)(4,1)}), s8[4194304]{0:T(1024)(128)(4,1)S(1)}, s32[]{:S(2)}) async-start(s8[8388608]{0:T(1024)(128)(4,1)} %bitcast.159), calls=%async_computation.4 | async-start | bytes 8388608
  219.2 23.3 %slice-start.1 = ((s8[8388608]{0:T(1024)(128)(4,1)}), s8[4194304]{0:T(1024)(128)(4,1)S(1)}, s32[]{:S(2)}) async-start(s8[8388608]{0:T(1024)(128)(4,1)} %bitcast.159), calls=%async_computation.5 | async-start | bytes 8388608
  224.4 18.1 %copy-start.9 = (f32[32,2048]{1,0:T(8,128)S(1)}, f32[32,2048]{1,0:T(8,128)}, u32[]{:S(2)}) copy-start(f32[32,2048]{1,0:T(8,128)} %param.16) | copy-start | bytes 786436
  227.4 6.6 %collective-permute-start.28 = (bf16[32,2048]{1,0:T(8,128)(2,1)S(1)}, bf16[32,2048]{1,0:T(8,128)(2,1)S(1)}, u32[]{:S(2)}, u32[]{:S(2)}) collective-permute-start(bf16[32,2048]{1,0:T(8,128)(2,1)S(1)} %constant_dynamic-update-slice_fusion.17), channel_id=1, source_target_pairs={{0,4},{1,5},{2,6},{3,7},{4,0},{5,1},{6,2},{7,3},{8,12},{9,13},{10,... | collective-permute-start | bytes 393224 | tf_op jit(solution)/shard_map/ppermute | solution.py:83
  234.0 6.3 %collective-permute-start.31 = (bf16[32,2048]{1,0:T(8,128)(2,1)S(1)}, bf16[32,2048]{1,0:T(8,128)(2,1)S(1)}, u32[]{:S(2)}, u32[]{:S(2)}) collective-permute-start(bf16[32,2048]{1,0:T(8,128)(2,1)S(1)} %add_convert_fusion.5), channel_id=1, source_target_pairs={{0,3},{1,2},{2,1},{3,0},{4,7},{5,6},{6,5},{7,4},{8,11},{9,10},{10,... | collective-permute-start | bytes 393224 | tf_op jit(solution)/shard_map/ppermute | solution.py:83
  235.4 6.5 %collective-permute-start.30 = (bf16[32,2048]{1,0:T(8,128)(2,1)S(1)}, bf16[32,2048]{1,0:T(8,128)(2,1)S(1)}, u32[]{:S(2)}, u32[]{:S(2)}) collective-permute-start(bf16[32,2048]{1,0:T(8,128)(2,1)S(1)} %add_convert_fusion.5), channel_id=1, source_target_pairs={{0,2},{1,3},{2,0},{3,1},{4,6},{5,7},{6,4},{7,5},{8,10},{9,11},{10,... | collective-permute-start | bytes 393224 | tf_op jit(solution)/shard_map/ppermute | solution.py:83
  236.2 6.3 %collective-permute-start.29 = (bf16[32,2048]{1,0:T(8,128)(2,1)S(1)}, bf16[32,2048]{1,0:T(8,128)(2,1)S(1)}, u32[]{:S(2)}, u32[]{:S(2)}) collective-permute-start(bf16[32,2048]{1,0:T(8,128)(2,1)S(1)} %add_convert_fusion.5), channel_id=1, source_target_pairs={{0,1},{1,0},{2,3},{3,2},{4,5},{5,4},{6,7},{7,6},{8,9},{9,8},{10,11... | collective-permute-start | bytes 393224 | tf_op jit(solution)/shard_map/ppermute | solution.py:83
  247.8 6.6 %collective-permute-start.32 = (bf16[32,2048]{1,0:T(8,128)(2,1)S(1)}, bf16[32,2048]{1,0:T(8,128)(2,1)S(1)}, u32[]{:S(2)}, u32[]{:S(2)}) collective-permute-start(bf16[32,2048]{1,0:T(8,128)(2,1)S(1)} %shard_map.109), channel_id=1, source_target_pairs={{0,4},{1,5},{2,6},{3,7},{4,0},{5,1},{6,2},{7,3},{8,12},{9,13},{10,... | collective-permute-start | bytes 393224 | tf_op jit(solution)/shard_map/ppermute | solution.py:83
  254.4 6.3 %collective-permute-start.35 = (bf16[32,2048]{1,0:T(8,128)(2,1)S(1)}, bf16[32,2048]{1,0:T(8,128)(2,1)S(1)}, u32[]{:S(2)}, u32[]{:S(2)}) collective-permute-start(bf16[32,2048]{1,0:T(8,128)(2,1)S(1)} %add_convert_fusion.3), channel_id=1, source_target_pairs={{0,3},{1,2},{2,1},{3,0},{4,7},{5,6},{6,5},{7,4},{8,11},{9,10},{10,... | collective-permute-start | bytes 393224 | tf_op jit(solution)/shard_map/ppermute | solution.py:83
  255.8 6.5 %collective-permute-start.34 = (bf16[32,2048]{1,0:T(8,128)(2,1)S(1)}, bf16[32,2048]{1,0:T(8,128)(2,1)S(1)}, u32[]{:S(2)}, u32[]{:S(2)}) collective-permute-start(bf16[32,2048]{1,0:T(8,128)(2,1)S(1)} %add_convert_fusion.3), channel_id=1, source_target_pairs={{0,2},{1,3},{2,0},{3,1},{4,6},{5,7},{6,4},{7,5},{8,10},{9,11},{10,... | collective-permute-start | bytes 393224 | tf_op jit(solution)/shard_map/ppermute | solution.py:83
  257.2 5.7 %collective-permute-start.33 = (bf16[32,2048]{1,0:T(8,128)(2,1)S(1)}, bf16[32,2048]{1,0:T(8,128)(2,1)S(1)}, u32[]{:S(2)}, u32[]{:S(2)}) collective-permute-start(bf16[32,2048]{1,0:T(8,128)(2,1)S(1)} %add_convert_fusion.3), channel_id=1, source_target_pairs={{0,1},{1,0},{2,3},{3,2},{4,5},{5,4},{6,7},{7,6},{8,9},{9,8},{10,11... | collective-permute-start | bytes 393224 | tf_op jit(solution)/shard_map/ppermute | solution.py:83
  (23 other events, 113.3 us)
